TPU v7x, 32 devices: a whole 2x2x4 slice. The times are simulated.
32 devices in a mesh: depth: 4 (over x, core), row: 4 (over z), col: 2 (over y).
Axes of the slice: x: 2, y: 2, z: 4, core: 2. Of those that a mesh axis runs over, the one named last changes fastest.
Arguments:
- density: float32 [4096, 4096], P('row', ('depth', 'col')), as said below
- pattern: int32 [64, 64], replicated, may hold values from 0 to 1, as said below
- filters: int32 [4, 64, 64], replicated, may hold values from 0 to 1, as said below
Outputs:
- purified: float32 [4096, 4096], P('row', ('depth', 'col'))
Inputs may be any that keep to these rules, and one draw needn't show every extreme that they name: density is symmetric. `pattern`: symmetric 0/1 block table with every diagonal block set. `filters`: each table is a symmetric 0/1 block table with every diagonal block set.
All inputs are finite; a program needn't handle non-finite values.
Results may differ from a plain program's by a relative error of at most 0.007.
Values may be sent and summed in bfloat16 or wider, within the bound.
A program may use at most 64 MiB of HBM per device.

v0:
```python
import jax
import jax.numpy as jnp
from jax import lax
from jax.sharding import PartitionSpec as P

BLK = 64
PURIFY = 2


def spread(value, axis, root):
    mine = lax.axis_index(axis) == root
    return lax.psum(jnp.where(mine, value, jnp.zeros_like(value)), axis)


def on_device(density, pattern, filters):
    rows_wide, seg_width = density.shape
    n_depth = lax.axis_size("depth")
    n_col = lax.axis_size("col")
    layer_index = lax.axis_index("depth")
    row_index = lax.axis_index("row")
    col_index = lax.axis_index("col")
    row_blocks = rows_wide // BLK
    seg_blocks = seg_width // BLK

    def full_mask(keep_table):
        row_strip = lax.dynamic_slice_in_dim(keep_table, row_index * row_blocks, row_blocks, 0)
        groups = row_strip.reshape(row_blocks, n_depth, n_col, seg_blocks)
        picked = lax.dynamic_slice_in_dim(groups, col_index, 1, 2)
        return picked.reshape(row_blocks, n_depth * seg_blocks).astype(jnp.float32)

    def own_mask(keep_table):
        return lax.dynamic_slice_in_dim(
            full_mask(keep_table), layer_index * seg_blocks, seg_blocks, 1
        )

    def apply_mask(values, keep_mask):
        row_count, col_count = keep_mask.shape
        shaped = values.reshape(row_count, BLK, col_count, BLK) * keep_mask[:, None, :, None]
        return shaped.reshape(values.shape)

    def multiply(left_tile, right_side):
        return jnp.dot(
            lax.all_gather(left_tile, "col", axis=1, tiled=True),
            right_side,
            preferred_element_type=jnp.float32,
        )

    def share_layers(partial_sum):
        return lax.psum_scatter(partial_sum, "depth", scatter_dimension=1, tiled=True)

    start_matrix = apply_mask(density, own_mask(pattern))
    current = start_matrix
    for round_index in range(PURIFY):
        operand = current.astype(jnp.bfloat16)
        right_side = spread(
            lax.all_gather(operand, "depth", axis=1, tiled=True), "row", layer_index
        )
        square = apply_mask(
            share_layers(multiply(operand, right_side)), own_mask(filters[2 * round_index])
        )
        cubic = apply_mask(
            share_layers(multiply(square.astype(jnp.bfloat16), right_side)),
            own_mask(filters[2 * round_index + 1]),
        )
        current = 3.0 * square - 2.0 * cubic
    return current


def solution(mesh):
    return jax.shard_map(
        on_device,
        mesh=mesh,
        in_specs=(P("row", ("depth", "col")), P(), P()),
        out_specs=P("row", ("depth", "col")),
        check_vma=False,
    )
```

profile of v0, /device:TPU:0, one launch (start us, length us, event | category | flops | bytes accessed | tf_op | source)
XLA Modules:
  0.0 889.9 jit_solution(13428316623293829066)
XLA Ops:
  16.9 36.5 %all-gather.9.cloned.1.call-done = bf16[1024,2048]{1,0:T(8,128)(2,1)} async-done(((bf16[1024,512]{1,0:T(8,128)(2,1)}), bf16[1024,2048]{1,0:T(8,128)(2,1)}) %all-gather.9.cloned.1.call-update) | async-done | bytes 4194320 | tf_op jit(solution)/shard_map/all_gather | solution.py:56
  53.5 4.5 broadcast_select_fusion.1
  58.0 30.2 %all-gather.7.cloned.1.call-done = bf16[1024,1024]{1,0:T(8,128)(2,1)} async-done(((bf16[1024,512]{1,0:T(8,128)(2,1)}), bf16[1024,1024]{1,0:T(8,128)(2,1)}) %all-gather.7.cloned.1.call-update) | async-done | bytes 2097168 | tf_op jit(solution)/shard_map/all_gather | solution.py:43
  88.2 157.4 %all-reduce.3.cloned.1.call-done = bf16[1024,2048]{1,0:T(8,128)(2,1)} async-done(((bf16[1024,2048]{1,0:T(8,128)(2,1)}), bf16[1024,2048]{1,0:T(8,128)(2,1)}) %all-reduce.3.cloned.1.call-update) | async-done | bytes 4194320 | tf_op jit(solution)/shard_map/psum | solution.py:12
  245.5 10.6 %fusion.1 = f32[1024,2048]{1,0:T(8,128)} fusion(bf16[1024,1024]{1,0:T(8,128)(2,1)} %all-gather.7.cloned.1.call-done, bf16[1024,2048]{1,0:T(8,128)(2,1)} %all-reduce.3.cloned.1.call-done), kind=kOutput, calls=%fused_computation.23 | convolution fusion | flops 4294967296 | bytes 14680064 | tf_op jit(solution)/shard_map/dot_general | solution.py:42
  259.5 3.8 mul.87
  263.3 63.7 %reduce-scatter.5.cloned.1.call-done = f32[1024,512]{1,0:T(8,128)} async-done(((f32[1024,2048]{1,0:T(8,128)}), f32[1024,512]{1,0:T(8,128)}) %reduce-scatter.5.cloned.1.call-update) | async-done | bytes 2097168 | tf_op jit(solution)/shard_map/reduce_scatter | solution.py:49
  330.0 33.2 %all-gather.11.cloned.1.call-done = bf16[1024,1024]{1,0:T(8,128)(2,1)} async-done(((bf16[1024,512]{1,0:T(8,128)(2,1)}), bf16[1024,1024]{1,0:T(8,128)(2,1)}) %all-gather.11.cloned.1.call-update) | async-done | bytes 2097168 | tf_op jit(solution)/shard_map/all_gather | solution.py:43
  363.2 10.6 %fusion.2 = f32[1024,2048]{1,0:T(8,128)} fusion(bf16[1024,1024]{1,0:T(8,128)(2,1)} %all-gather.11.cloned.1.call-done, bf16[1024,2048]{1,0:T(8,128)(2,1)} %all-reduce.3.cloned.1.call-done), kind=kOutput, calls=%fused_computation.24 | convolution fusion | flops 4294967296 | bytes 14680064 | tf_op jit(solution)/shard_map/dot_general | solution.py:42
  376.6 5.0 mul.91
  381.6 64.1 %reduce-scatter.7.cloned.1.call-done = f32[1024,512]{1,0:T(8,128)} async-done(((f32[1024,2048]{1,0:T(8,128)}), f32[1024,512]{1,0:T(8,128)}) %reduce-scatter.7.cloned.1.call-update) | async-done | bytes 2097168 | tf_op jit(solution)/shard_map/reduce_scatter | solution.py:49
  445.7 4.9 subtract_convert_fusion
  451.5 33.8 %all-gather.15.cloned.1.call-done = bf16[1024,2048]{1,0:T(8,128)(2,1)} async-done(((bf16[1024,512]{1,0:T(8,128)(2,1)}), bf16[1024,2048]{1,0:T(8,128)(2,1)}) %all-gather.15.cloned.1.call-update) | async-done | bytes 4194320 | tf_op jit(solution)/shard_map/all_gather | solution.py:56
  485.3 4.4 broadcast_select_fusion
  489.8 30.3 %all-gather.13.cloned.1.call-done = bf16[1024,1024]{1,0:T(8,128)(2,1)} async-done(((bf16[1024,512]{1,0:T(8,128)(2,1)}), bf16[1024,1024]{1,0:T(8,128)(2,1)}) %all-gather.13.cloned.1.call-update) | async-done | bytes 2097168 | tf_op jit(solution)/shard_map/all_gather | solution.py:43
  520.1 157.5 %all-reduce.5.cloned.1.call-done = bf16[1024,2048]{1,0:T(8,128)(2,1)} async-done(((bf16[1024,2048]{1,0:T(8,128)(2,1)}), bf16[1024,2048]{1,0:T(8,128)(2,1)}) %all-reduce.5.cloned.1.call-update) | async-done | bytes 4194320 | tf_op jit(solution)/shard_map/psum | solution.py:12
  677.6 10.6 %fusion.3 = f32[1024,2048]{1,0:T(8,128)} fusion(bf16[1024,1024]{1,0:T(8,128)(2,1)} %all-gather.13.cloned.1.call-done, bf16[1024,2048]{1,0:T(8,128)(2,1)} %all-reduce.5.cloned.1.call-done), kind=kOutput, calls=%fused_computation.25 | convolution fusion | flops 4294967296 | bytes 14680064 | tf_op jit(solution)/shard_map/dot_general | solution.py:42
  690.7 3.5 mul.95
  694.3 64.9 %reduce-scatter.9.cloned.1.call-done = f32[1024,512]{1,0:T(8,128)} async-done(((f32[1024,2048]{1,0:T(8,128)}), f32[1024,512]{1,0:T(8,128)}) %reduce-scatter.9.cloned.1.call-update) | async-done | bytes 2097168 | tf_op jit(solution)/shard_map/reduce_scatter | solution.py:49
  762.3 33.0 %all-gather.17.cloned.1.call-done = bf16[1024,1024]{1,0:T(8,128)(2,1)} async-done(((bf16[1024,512]{1,0:T(8,128)(2,1)}), bf16[1024,1024]{1,0:T(8,128)(2,1)}) %all-gather.17.cloned.1.call-update) | async-done | bytes 2097168 | tf_op jit(solution)/shard_map/all_gather | solution.py:43
  795.3 10.6 %fusion.4 = f32[1024,2048]{1,0:T(8,128)} fusion(bf16[1024,1024]{1,0:T(8,128)(2,1)} %all-gather.17.cloned.1.call-done, bf16[1024,2048]{1,0:T(8,128)(2,1)} %all-reduce.5.cloned.1.call-done), kind=kOutput, calls=%fused_computation.26 | convolution fusion | flops 4294967296 | bytes 14680064 | tf_op jit(solution)/shard_map/dot_general | solution.py:42
  808.4 5.0 mul.99
  813.4 64.4 %reduce-scatter.11.cloned.1.call-done = f32[1024,512]{1,0:T(8,128)} async-done(((f32[1024,2048]{1,0:T(8,128)}), f32[1024,512]{1,0:T(8,128)}) %reduce-scatter.11.cloned.1.call-update) | async-done | bytes 2097168 | tf_op jit(solution)/shard_map/reduce_scatter | solution.py:49
  877.8 5.2 multiply_subtract_fusion
  (63 shorter events, 28.5 us)
Async XLA Ops:
  6.5 0.8 copy-start
  6.5 46.9 %all-gather.9.cloned.1.call-start = ((), (), s32[]{:S(2)}) async-start(), calls=%async_computation.5 | async-start | bytes 5242880 | tf_op jit(solution)/shard_map/all_gather | solution.py:56
  16.1 72.0 %all-gather.7.cloned.1.call-start = ((), (), s32[]{:S(2)}) async-start(), calls=%async_computation.4 | async-start | bytes 3145728 | tf_op jit(solution)/shard_map/all_gather | solution.py:43
  16.9 228.7 %all-reduce.3.cloned.1.call-start = ((), (), s32[]{:S(2)}) async-start(), calls=%async_computation.6 | async-start | bytes 8388608 | tf_op jit(solution)/shard_map/psum | solution.py:12
  57.9 269.1 %reduce-scatter.5.cloned.1.call-start = ((), (), s32[]{:S(2)}) async-start(), calls=%async_computation.7 | async-start | bytes 10485760 | tf_op jit(solution)/shard_map/reduce_scatter | solution.py:49
  256.1 0.9 copy-start.2
  256.1 107.1 %all-gather.11.cloned.1.call-start = ((), (), s32[]{:S(2)}) async-start(), calls=%async_computation.8 | async-start | bytes 3145728 | tf_op jit(solution)/shard_map/all_gather | solution.py:43
  329.9 115.8 %reduce-scatter.7.cloned.1.call-start = ((), (), s32[]{:S(2)}) async-start(), calls=%async_computation.9 | async-start | bytes 10485760 | tf_op jit(solution)/shard_map/reduce_scatter | solution.py:49
  373.8 111.5 %all-gather.15.cloned.1.call-start = ((), (), s32[]{:S(2)}) async-start(), calls=%async_computation.11 | async-start | bytes 5242880 | tf_op jit(solution)/shard_map/all_gather | solution.py:56
  450.7 69.4 %all-gather.13.cloned.1.call-start = ((), (), s32[]{:S(2)}) async-start(), calls=%async_computation.10 | async-start | bytes 3145728 | tf_op jit(solution)/shard_map/all_gather | solution.py:43
  451.4 226.2 %all-reduce.5.cloned.1.call-start = ((), (), s32[]{:S(2)}) async-start(), calls=%async_computation.12 | async-start | bytes 8388608 | tf_op jit(solution)/shard_map/psum | solution.py:12
  489.8 269.4 %reduce-scatter.9.cloned.1.call-start = ((), (), s32[]{:S(2)}) async-start(), calls=%async_computation.13 | async-start | bytes 10485760 | tf_op jit(solution)/shard_map/reduce_scatter | solution.py:49
  688.2 107.1 %all-gather.17.cloned.1.call-start = ((), (), s32[]{:S(2)}) async-start(), calls=%async_computation.14 | async-start | bytes 3145728 | tf_op jit(solution)/shard_map/all_gather | solution.py:43
  762.1 115.8 %reduce-scatter.11.cloned.1.call-start = ((), (), s32[]{:S(2)}) async-start(), calls=%async_computation.15 | async-start | bytes 10485760 | tf_op jit(solution)/shard_map/reduce_scatter | solution.py:49
  877.8 5.2 copy-start.1
Sparse Core Ops, SparseCore 0:
  16.2 37.1 all-gather.8
  55.0 33.1 all-gather.6
  90.5 154.9 all-reduce.2
  256.3 70.7 reduce-scatter.4
  330.1 33.1 all-gather.10
  373.9 71.7 reduce-scatter.6
  450.8 34.4 all-gather.14
  486.9 33.1 all-gather.12
  522.6 154.9 all-reduce.4
  688.3 70.7 reduce-scatter.8
  762.2 33.1 all-gather.16
  806.1 71.7 reduce-scatter.10
where the time goes:
time: 891 us; the launch traced here: 890 us
  waiting for transfers between devices  771 us (87%)
  matrix products  42.3 us (5%)
  local copies, waits for them, and re-layouts  34.7 us (4%)
  other arithmetic  27.8 us (3%)
  between operations  13.7 us (2%)
    psum x2, waiting for transfers between devices, spread(): return lax.psum(jnp.where(mine, value, jnp.zeros_like(value)), axis)  315 us
    reduce_scatter x4, waiting for transfers between devices, share_layers(): lax.psum_scatter(partial_sum, 'depth', scatter_dimension=1, tiled=True)  257 us
    all_gather x4, waiting for transfers between devices, multiply(): lax.all_gather(left_tile, 'col', axis=1, tiled=True)  127 us
    all_gather x2, waiting for transfers between devices, on_device(): lax.all_gather(operand, 'depth', axis=1, tiled=True)  70.4 us
    dot_general x4, matrix products, multiply(): jnp.dot(lax.all_gather(left_tile, 'col', axis=1, tiled=True), right_side,...  42.3 us
    mul x10, local copies, waits for them, and re-layouts, apply_mask(): values.reshape(row_count, BLK, col_count, BLK) * keep_mask[:, None, :, None]  32.3 us
  transfers between devices with their start and end apart: 12, of which 12 were waited for; matrix products, arithmetic and copies ran while one was open for 4% of the time, Pallas kernels for 0%

commit v1 on v0

--- a/solution.py
+++ b/solution.py
@@ -5,6 +5,18 @@
 
 BLK = 64
 PURIFY = 2
+
+
+def find_figure(frame_in, link_axis):
+    high, r1 = (lax.psum(1, link_axis), lax.axis_index(link_axis))
+    d_next, y2 = (frame_in, 1)
+    while y2 < high:
+        low = lax.ppermute(d_next, link_axis, [(dev_j, dev_j ^ y2) for dev_j in range(high)])
+        vec_out = jnp.concatenate([d_next, low], axis=1)
+        found_now = jnp.concatenate([low, d_next], axis=1)
+        d_next = jnp.where(r1 & y2 == 0, vec_out, found_now)
+        y2 = 2 * y2
+    return d_next
 
 
 def spread(value, axis, root):
@@ -52,9 +64,7 @@
     current = start_matrix
     for round_index in range(PURIFY):
         operand = current.astype(jnp.bfloat16)
-        right_side = spread(
-            lax.all_gather(operand, "depth", axis=1, tiled=True), "row", layer_index
-        )
+        right_side = spread(find_figure(operand, "depth"), "row", layer_index)
         square = apply_mask(
             share_layers(multiply(operand, right_side)), own_mask(filters[2 * round_index])
         )

time: 891 us -> 861 us (0.966)
  waiting for transfers between devices: 771 us -> 733 us
    ppermute x0 -> x4, waiting for transfers between devices: none -> 98.4 us  [find_figure(): lax.ppermute(d_next, link_axis, [(dev_j, dev_j ^ y2) for dev_j in range(h...]
    all_gather x2 -> x0, waiting for transfers between devices: 70.4 us -> none  [on_device(): lax.all_gather(operand, 'depth', axis=1, tiled=True)]
    all_gather x4, waiting for transfers between devices: 127 us -> 66.3 us  [multiply(): lax.all_gather(left_tile, 'col', axis=1, tiled=True)]
  transfers between devices with their start and end apart: 12 -> 14, of which waited for: 12 -> 12; matrix products, arithmetic and copies ran while one was open for 4% -> 4% of each run, Pallas kernels for 0% -> 0%
where the time goes in v1:
time: 861 us; the launch traced here: 860 us
  waiting for transfers between devices  733 us (85%)
  matrix products  42.3 us (5%)
  local copies, waits for them, and re-layouts  34.7 us (4%)
  other arithmetic  30.2 us (4%)
  between operations  15.1 us (2%)
    psum x2, waiting for transfers between devices, spread(): return lax.psum(jnp.where(mine, value, jnp.zeros_like(value)), axis)  311 us
    reduce_scatter x4, waiting for transfers between devices, share_layers(): lax.psum_scatter(partial_sum, 'depth', scatter_dimension=1, tiled=True)  257 us
    ppermute x4, waiting for transfers between devices, find_figure(): lax.ppermute(d_next, link_axis, [(dev_j, dev_j ^ y2) for dev_j in range(h...  98.4 us
    all_gather x4, waiting for transfers between devices, multiply(): lax.all_gather(left_tile, 'col', axis=1, tiled=True)  66.3 us
    dot_general x4, matrix products, multiply(): jnp.dot(lax.all_gather(left_tile, 'col', axis=1, tiled=True), right_side,...  42.3 us
    mul x10, local copies, waits for them, and re-layouts, apply_mask(): values.reshape(row_count, BLK, col_count, BLK) * keep_mask[:, None, :, None]  32.3 us
  transfers between devices with their start and end apart: 14, of which 12 were waited for; matrix products, arithmetic and copies ran while one was open for 4% of the time, Pallas kernels for 0%

profile of v1, /device:TPU:0, one launch (start us, length us, event | category | flops | bytes accessed | tf_op | source)
XLA Modules:
  0.0 860.1 jit_solution(1468699436418513954)
XLA Ops:
  10.6 3.4 mul.84
  21.2 2.9 collective-permute-start.1
  24.2 46.0 %collective-permute-done.1 = bf16[1024,1024]{1,0:T(8,128)(2,1)} collective-permute-done((bf16[1024,1024]{1,0:T(8,128)(2,1)S(1)}, bf16[1024,1024]{1,0:T(8,128)(2,1)}, u32[]{:S(2)}, u32[]{:S(2)}) %collective-permute-start.1) | collective-permute-done | bytes 2097184 | tf_op jit(solution)/shard_map/ppermute | solution.py:14
  70.2 5.2 fusion
  75.5 156.3 %all-reduce.3.cloned.1.call-done = bf16[1024,2048]{1,0:T(8,128)(2,1)} async-done(((bf16[1024,2048]{1,0:T(8,128)(2,1)}), bf16[1024,2048]{1,0:T(8,128)(2,1)}) %all-reduce.3.cloned.1.call-update) | async-done | bytes 4194320 | tf_op jit(solution)/shard_map/psum | solution.py:24
  231.8 10.6 %fusion.3 = f32[1024,2048]{1,0:T(8,128)} fusion(bf16[1024,1024]{1,0:T(8,128)(2,1)} %all-gather.5.cloned.1.call-done, bf16[1024,2048]{1,0:T(8,128)(2,1)} %all-reduce.3.cloned.1.call-done), kind=kOutput, calls=%fused_computation.27 | convolution fusion | flops 4294967296 | bytes 14680064 | tf_op jit(solution)/shard_map/dot_general | solution.py:54
  245.7 3.8 mul.87
  249.5 63.7 %reduce-scatter.5.cloned.1.call-done = f32[1024,512]{1,0:T(8,128)} async-done(((f32[1024,2048]{1,0:T(8,128)}), f32[1024,512]{1,0:T(8,128)}) %reduce-scatter.5.cloned.1.call-update) | async-done | bytes 2097168 | tf_op jit(solution)/shard_map/reduce_scatter | solution.py:61
  316.2 33.2 %all-gather.7.cloned.1.call-done = bf16[1024,1024]{1,0:T(8,128)(2,1)} async-done(((bf16[1024,512]{1,0:T(8,128)(2,1)}), bf16[1024,1024]{1,0:T(8,128)(2,1)}) %all-gather.7.cloned.1.call-update) | async-done | bytes 2097168 | tf_op jit(solution)/shard_map/all_gather | solution.py:55
  349.5 10.6 %fusion.4 = f32[1024,2048]{1,0:T(8,128)} fusion(bf16[1024,1024]{1,0:T(8,128)(2,1)} %all-gather.7.cloned.1.call-done, bf16[1024,2048]{1,0:T(8,128)(2,1)} %all-reduce.3.cloned.1.call-done), kind=kOutput, calls=%fused_computation.28 | convolution fusion | flops 4294967296 | bytes 14680064 | tf_op jit(solution)/shard_map/dot_general | solution.py:54
  362.8 5.0 mul.91
  367.8 64.1 %reduce-scatter.7.cloned.1.call-done = f32[1024,512]{1,0:T(8,128)} async-done(((f32[1024,2048]{1,0:T(8,128)}), f32[1024,512]{1,0:T(8,128)}) %reduce-scatter.7.cloned.1.call-update) | async-done | bytes 2097168 | tf_op jit(solution)/shard_map/reduce_scatter | solution.py:61
  432.0 3.9 subtract_convert_fusion
  439.7 47.4 %collective-permute-done.3 = bf16[1024,1024]{1,0:T(8,128)(2,1)} collective-permute-done((bf16[1024,1024]{1,0:T(8,128)(2,1)S(1)}, bf16[1024,1024]{1,0:T(8,128)(2,1)}, u32[]{:S(2)}, u32[]{:S(2)}) %collective-permute-start.3) | collective-permute-done | bytes 2097184 | tf_op jit(solution)/shard_map/ppermute | solution.py:14
  487.1 5.2 fusion.1
  492.4 154.8 %all-reduce.5.cloned.1.call-done = bf16[1024,2048]{1,0:T(8,128)(2,1)} async-done(((bf16[1024,2048]{1,0:T(8,128)(2,1)}), bf16[1024,2048]{1,0:T(8,128)(2,1)}) %all-reduce.5.cloned.1.call-update) | async-done | bytes 4194320 | tf_op jit(solution)/shard_map/psum | solution.py:24
  647.2 10.6 %fusion.5 = f32[1024,2048]{1,0:T(8,128)} fusion(bf16[1024,1024]{1,0:T(8,128)(2,1)} %all-gather.9.cloned.1.call-done, bf16[1024,2048]{1,0:T(8,128)(2,1)} %all-reduce.5.cloned.1.call-done), kind=kOutput, calls=%fused_computation.29 | convolution fusion | flops 4294967296 | bytes 14680064 | tf_op jit(solution)/shard_map/dot_general | solution.py:54
  660.4 3.5 mul.95
  663.9 64.9 %reduce-scatter.9.cloned.1.call-done = f32[1024,512]{1,0:T(8,128)} async-done(((f32[1024,2048]{1,0:T(8,128)}), f32[1024,512]{1,0:T(8,128)}) %reduce-scatter.9.cloned.1.call-update) | async-done | bytes 2097168 | tf_op jit(solution)/shard_map/reduce_scatter | solution.py:61
  732.0 33.0 %all-gather.11.cloned.1.call-done = bf16[1024,1024]{1,0:T(8,128)(2,1)} async-done(((bf16[1024,512]{1,0:T(8,128)(2,1)}), bf16[1024,1024]{1,0:T(8,128)(2,1)}) %all-gather.11.cloned.1.call-update) | async-done | bytes 2097168 | tf_op jit(solution)/shard_map/all_gather | solution.py:55
  765.0 10.6 %fusion.6 = f32[1024,2048]{1,0:T(8,128)} fusion(bf16[1024,1024]{1,0:T(8,128)(2,1)} %all-gather.11.cloned.1.call-done, bf16[1024,2048]{1,0:T(8,128)(2,1)} %all-reduce.5.cloned.1.call-done), kind=kOutput, calls=%fused_computation.30 | convolution fusion | flops 4294967296 | bytes 14680064 | tf_op jit(solution)/shard_map/dot_general | solution.py:54
  778.1 5.0 mul.99
  783.0 64.4 %reduce-scatter.11.cloned.1.call-done = f32[1024,512]{1,0:T(8,128)} async-done(((f32[1024,2048]{1,0:T(8,128)}), f32[1024,512]{1,0:T(8,128)}) %reduce-scatter.11.cloned.1.call-update) | async-done | bytes 2097168 | tf_op jit(solution)/shard_map/reduce_scatter | solution.py:61
  847.4 5.2 multiply_subtract_fusion
  (71 shorter events, 31.7 us)
Async XLA Ops:
  7.4 0.8 copy-start
  7.4 68.1 %all-gather.5.cloned.1.call-start = ((), (), s32[]{:S(2)}) async-start(), calls=%async_computation.4 | async-start | bytes 3145728 | tf_op jit(solution)/shard_map/all_gather | solution.py:55
  16.0 5.2 copy-start.2
  16.0 2.9 collective-permute-start
  21.2 49.0 %collective-permute-start.1 = (bf16[1024,1024]{1,0:T(8,128)(2,1)S(1)}, bf16[1024,1024]{1,0:T(8,128)(2,1)}, u32[]{:S(2)}, u32[]{:S(2)}) collective-permute-start(bf16[1024,1024]{1,0:T(8,128)(2,1)S(1)} %maximum_select_fusion.2), channel_id=1, source_target_pairs={{0,16},{8,24},{16,0},{24,8},{1,17},{9,25},{17,1},{25,9},{2,18},{10... | collective-permute-start | bytes 6291464 | tf_op jit(solution)/shard_map/ppermute | solution.py:14
  24.2 207.6 %all-reduce.3.cloned.1.call-start = ((), (), s32[]{:S(2)}) async-start(), calls=%async_computation.5 | async-start | bytes 8388608 | tf_op jit(solution)/shard_map/psum | solution.py:24
  75.4 237.9 %reduce-scatter.5.cloned.1.call-start = ((), (), s32[]{:S(2)}) async-start(), calls=%async_computation.6 | async-start | bytes 10485760 | tf_op jit(solution)/shard_map/reduce_scatter | solution.py:61
  242.3 0.9 copy-start.4
  242.4 107.1 %all-gather.7.cloned.1.call-start = ((), (), s32[]{:S(2)}) async-start(), calls=%async_computation.7 | async-start | bytes 3145728 | tf_op jit(solution)/shard_map/all_gather | solution.py:55
  316.2 115.8 %reduce-scatter.7.cloned.1.call-start = ((), (), s32[]{:S(2)}) async-start(), calls=%async_computation.8 | async-start | bytes 10485760 | tf_op jit(solution)/shard_map/reduce_scatter | solution.py:61
  360.0 132.4 %all-gather.9.cloned.1.call-start = ((), (), s32[]{:S(2)}) async-start(), calls=%async_computation.9 | async-start | bytes 3145728 | tf_op jit(solution)/shard_map/all_gather | solution.py:55
  435.9 3.4 copy-start.3
  435.9 2.7 collective-permute-start.2
  439.3 47.8 %collective-permute-start.3 = (bf16[1024,1024]{1,0:T(8,128)(2,1)S(1)}, bf16[1024,1024]{1,0:T(8,128)(2,1)}, u32[]{:S(2)}, u32[]{:S(2)}) collective-permute-start(bf16[1024,1024]{1,0:T(8,128)(2,1)S(1)} %maximum_select_fusion.3), channel_id=1, source_target_pairs={{0,16},{8,24},{16,0},{24,8},{1,17},{9,25},{17,1},{25,9},{2,18},{10... | collective-permute-start | bytes 6291464 | tf_op jit(solution)/shard_map/ppermute | solution.py:14
  439.7 207.5 %all-reduce.5.cloned.1.call-start = ((), (), s32[]{:S(2)}) async-start(), calls=%async_computation.10 | async-start | bytes 8388608 | tf_op jit(solution)/shard_map/psum | solution.py:24
  492.3 236.4 %reduce-scatter.9.cloned.1.call-start = ((), (), s32[]{:S(2)}) async-start(), calls=%async_computation.11 | async-start | bytes 10485760 | tf_op jit(solution)/shard_map/reduce_scatter | solution.py:61
  657.8 107.1 %all-gather.11.cloned.1.call-start = ((), (), s32[]{:S(2)}) async-start(), calls=%async_computation.12 | async-start | bytes 3145728 | tf_op jit(solution)/shard_map/all_gather | solution.py:55
  731.7 115.8 %reduce-scatter.11.cloned.1.call-start = ((), (), s32[]{:S(2)}) async-start(), calls=%async_computation.13 | async-start | bytes 10485760 | tf_op jit(solution)/shard_map/reduce_scatter | solution.py:61
  847.4 5.2 copy-start.1
Sparse Core Ops, SparseCore 0:
  24.3 33.4 all-gather.4
  242.5 70.7 reduce-scatter.4
  316.3 33.1 all-gather.6
  360.2 71.7 reduce-scatter.6
  439.8 34.2 all-gather.8
  657.9 70.7 reduce-scatter.8
  731.8 33.1 all-gather.10
  775.7 71.7 reduce-scatter.10
Sparse Core Ops, SparseCore 1:
  75.5 156.2 all-reduce.2
  492.4 154.8 all-reduce.4
